TPU v7x, 32 devices: a whole 2x2x4 slice. The times are simulated.
32 devices in a mesh: seq: 8 (over z, x), head: 4 (over y, core).
Axes of the slice: x: 2, y: 2, z: 4, core: 2. Of those that a mesh axis runs over, the one named last changes fastest.
Arguments:
- queries: bfloat16 [4096, 1024], P('seq', 'head'), may hold values from -6 to 6
- keys: bfloat16 [4096, 1024], P('seq', 'head'), may hold values from -5 to 5
- values: bfloat16 [4096, 1024], P('seq', 'head'), may hold values from -6 to 6
- ridge: float32 [8], P('head'), may hold values from 0.5 to 4
- gain: float32 [1024], P('head'), may hold values from 0.5 to 1.5
- grad_out: bfloat16 [4096, 1024], P('seq', 'head'), may hold values from -6 to 6
Outputs:
- output: bfloat16 [4096, 1024], P('seq', 'head')
- grad_queries: bfloat16 [4096, 1024], P('seq', 'head')
- grad_keys: bfloat16 [4096, 1024], P('seq', 'head')
- grad_values: bfloat16 [4096, 1024], P('seq', 'head')
- grad_gain: float32 [1024], P('head')
All inputs are finite; a program needn't handle non-finite values.
Results may differ from a plain program's by a relative error of at most 0.0044.
Values sent between devices are 32-bit elements; how exact they have to be, the bound alone decides.
A program may use at most 64 MiB of HBM per device.

v0:
```python
import functools

import jax
import jax.numpy as jnp
from jax import lax
from jax.experimental import pallas as pl
from jax.experimental.pallas import tpu as pltpu
from jax.sharding import PartitionSpec as P

D = 128
CG_STEPS = 6
EPS = 1e-06
BLOCK_ROWS = 256
MESH = pl.DeviceIdType.MESH
F32 = jnp.float32
BF16 = jnp.bfloat16


def split(x):
    high = x.astype(BF16)
    return high, (x - high.astype(F32)).astype(BF16)


def dot(left, right):
    return jnp.dot(left, right, preferred_element_type=F32)


def dot_rows(left, right):
    return lax.dot_general(left, right, (((1,), (1,)), ((), ())), preferred_element_type=F32)


def side(pair):
    return jnp.concatenate(pair, axis=1)


def dot3(left, right):
    return dot(left[0], right[0]) + dot(left[1], right[0]) + dot(left[0], right[1])


def iotas(rows, cols):
    return (
        lax.broadcasted_iota(jnp.int32, (rows, cols), 0),
        lax.broadcasted_iota(jnp.int32, (rows, cols), 1),
    )


class Scan:
    def __init__(self, n, send, recv, excl, ssem, rsem, later):
        self.rounds = send.shape[0]
        self.send, self.recv, self.excl = send, recv, excl
        self.ssem, self.rsem, self.later = ssem, rsem, later
        self.me = lax.axis_index("seq")

    def partner(self, r):
        dist = 2**r
        bit = lax.rem(lax.div(self.me, dist), 2)
        return self.me + dist * (1 - 2 * bit), bit

    def copy(self, r):
        return pltpu.make_async_remote_copy(
            src_ref=self.send.at[r],
            dst_ref=self.recv.at[r],
            send_sem=self.ssem.at[r],
            recv_sem=self.rsem.at[r],
            device_id={"seq": self.partner(r)[0]},
            device_id_type=MESH,
        )

    def start(self, r):
        self.copy(r).start()

    def finish(self, r):
        self.copy(r).wait()
        _, bit = self.partner(r)
        weight = (1 - bit if self.later else bit).astype(F32)
        got = self.recv[r]
        part = weight * got
        self.excl[...] = part if r == 0 else self.excl[...] + part
        if r + 1 < self.rounds:
            self.send[r + 1] = self.send[r] + got
            self.start(r + 1)

    def total(self):
        return self.send[self.rounds - 1] + self.recv[self.rounds - 1]


def pack_sym(mats):
    if len(mats) % 2:
        return mats
    rows, cols = iotas(D, D)
    out = []
    for a, b in zip(mats[::2], mats[1::2]):
        out.append(jnp.where(rows < cols, a, b))
        diag = jnp.sum(jnp.where(rows == cols, a, 0.0), axis=0, keepdims=True)
        out.append(jnp.broadcast_to(diag, (8, D)))
    return out


def unpack_sym(ref, heads):
    if heads % 2:
        return [ref[pl.ds(h * D, D), :] for h in range(heads)]
    rows, cols = iotas(D, D)
    out = []
    for i in range(heads // 2):
        packed = ref[pl.ds(i * (D + 8), D), :]
        diag = ref[pl.ds(i * (D + 8) + D, 8), :][0:1, :]
        turned = packed.T
        a = jnp.where(rows == cols, diag, jnp.where(rows < cols, packed, turned))
        b = jnp.where(rows >= cols, packed, turned)
        out += [a, b]
    return out


def sym_rows(heads):
    return heads * D if heads % 2 else (heads // 2) * (D + 8)


def put(ref, parts):
    at = 0
    for part in parts:
        ref[0, pl.ds(at, part.shape[0]), :] = part
        at += part.shape[0]


def kernel(
    n_seq, n_head, heads, tok,
    q_ref, k_ref, v_ref, ridge_ref, gain_ref, up_ref,
    out_ref, gq_ref, gk_ref, gv_ref, gg_ref,
    kt2, vt2, k2, gram_h, gram_l,
    x_s, r_s, p_s, n_s, solved, mixed, gmix, gk_loc, gv_loc,
    gs, gr, ge, as_, ar, ae, ss, sr, se, ps, pr, pe,
    hs, hr,
    sem_s, sem_r, hsem_s, hsem_r,
):
    rows_blk = BLOCK_ROWS
    blocks = tok // rows_blk
    chains = [(h, b) for h in range(heads) for b in range(blocks)]
    scan_g = Scan(n_seq, gs, gr, ge, sem_s.at[0], sem_r.at[0], False)
    scan_a = Scan(n_seq, as_, ar, ae, sem_s.at[1], sem_r.at[1], False)
    scan_s = Scan(n_seq, ss, sr, se, sem_s.at[2], sem_r.at[2], True)
    scan_p = Scan(n_seq, ps, pr, pe, sem_s.at[3], sem_r.at[3], True)
    rounds = scan_g.rounds
    my_head = lax.axis_index("head")

    barrier = pltpu.get_barrier_semaphore()
    for r in range(rounds):
        pl.semaphore_signal(barrier, inc=1, device_id={"seq": scan_g.partner(r)[0]}, device_id_type=MESH)
    for j in range(1, n_head):
        pl.semaphore_signal(
            barrier, inc=1, device_id={"head": lax.rem(my_head + j, n_head)}, device_id_type=MESH
        )

    def tile(h, b):
        return (pl.ds(b * rows_blk, rows_blk), pl.ds(h * D, D))

    gram_blk, assoc_blk = {}, {}
    for c, (h, b) in enumerate(chains):
        key = k_ref[tile(h, b)]
        value = v_ref[tile(h, b)]
        key_t = key.astype(F32).T.astype(BF16)
        value_t = value.astype(F32).T.astype(BF16)
        kt2[c] = jnp.concatenate([key_t, key_t], axis=0)
        vt2[c] = jnp.concatenate([value_t, value_t], axis=0)
        k2[c] = side([key, key])
        both = dot(key_t, side([key, value]))
        gram_blk[h, b], assoc_blk[h, b] = both[:, :D], both[:, D:]
    put(gs, pack_sym([sum(gram_blk[h, b] for b in range(blocks)) for h in range(heads)]))
    pl.semaphore_wait(barrier, rounds + n_head - 1)
    scan_g.start(0)
    put(as_, [sum(assoc_blk[h, b] for b in range(blocks)) for h in range(heads)])

    def start_cg(c, rhs):
        x_s[c] = jnp.zeros_like(rhs)
        r_s[c] = rhs
        p_s[c] = rhs
        n_s[c] = jnp.broadcast_to(jnp.sum(rhs * rhs, axis=-1, keepdims=True), rhs.shape)

    for c, (h, b) in enumerate(chains):
        start_cg(c, q_ref[tile(h, b)].astype(F32))
    for r in range(rounds):
        scan_g.finish(r)
    scan_a.start(0)
    grams = unpack_sym(ge, heads)
    for h in range(heads):
        run = grams[h]
        for b in range(blocks):
            high, low = split(run)
            c = h * blocks + b
            gram_h[c] = jnp.concatenate([high, high], axis=0)
            gram_l[c] = low
            run = run + gram_blk[h, b]

    ri, ci = iotas(rows_blk, rows_blk)
    lower = ri >= ci
    upper = ri <= ci

    def cg_step(c, h, b):
        p = p_s[c]
        pair = split(p)
        p2 = side(pair)
        key = k_ref[tile(h, b)]
        score = split(jnp.where(lower, dot(p2, kt2[c]), 0.0))
        image = (
            dot(p2, gram_h[c]) + dot(pair[0], gram_l[c])
            + dot(score[0], key) + dot(score[1], key) + ridge_ref[h] * p
        )
        now = n_s[c]
        alpha = now / (jnp.sum(p * image, axis=-1, keepdims=True) + EPS)
        x_s[c] = x_s[c] + alpha * p
        res = r_s[c] - alpha * image
        new = jnp.broadcast_to(jnp.sum(res * res, axis=-1, keepdims=True), p.shape)
        r_s[c] = res
        n_s[c] = new
        p_s[c] = res + new / (now + EPS) * p

    spacing = max(CG_STEPS // rounds, 1)

    def solve(scan):
        def step_fn(step, carry):
            for c, (h, b) in enumerate(chains):
                cg_step(c, h, b)
            for r in range(rounds):
                if spacing * (r + 1) <= CG_STEPS:

                    @pl.when(step == spacing * (r + 1) - 1)
                    def _():
                        scan.finish(r)

            return carry

        lax.fori_loop(0, CG_STEPS, step_fn, 0)
        for r in range(rounds):
            if spacing * (r + 1) > CG_STEPS:
                scan.finish(r)

    solve(scan_a)

    assoc_all = {}
    for h in range(heads):
        run = ae[pl.ds(h * D, D), :]
        for b in range(blocks):
            c = h * blocks + b
            assoc_all[h, b] = run
            x = x_s[c]
            solved[c] = x
            pair = split(x)
            value = v_ref[tile(h, b)]
            score = split(jnp.where(lower, dot(side(pair), kt2[c]), 0.0))
            mixed[c] = dot3(pair, split(run)) + dot(score[0], value) + dot(score[1], value)
            run = run + assoc_blk[h, b]

    ones = jnp.ones((16, D), BF16)
    for b in range(blocks):
        square = jnp.zeros((16, rows_blk), F32)
        centre = jnp.zeros((16, rows_blk), F32)
        for h in range(heads):
            m = mixed[h * blocks + b]
            gain = gain_ref[:, pl.ds(h * D, D)]
            up = up_ref[tile(h, b)].astype(F32)
            for part in split(m * m):
                square = square + dot_rows(ones, part)
            for part in split(gain * up * m):
                centre = centre + dot_rows(ones, part)
        row, _ = iotas(8, rows_blk)
        hs[:, pl.ds(b * rows_blk, rows_blk)] = jnp.where(row < 4, square[:8], centre[:8])

    def head_copy(j):
        return pltpu.make_async_remote_copy(
            src_ref=hs,
            dst_ref=hr.at[j - 1],
            send_sem=hsem_s.at[j - 1],
            recv_sem=hsem_r.at[j - 1],
            device_id={"head": lax.rem(my_head + j, n_head)},
            device_id_type=MESH,
        )

    for j in range(1, n_head):
        head_copy(j).start()
    for j in range(1, n_head):
        head_copy(j).wait()
    sums = hs[...]
    for j in range(1, n_head):
        sums = sums + hr[j - 1]
    width = n_head * heads * D
    gain_rows = [jnp.zeros((8, D), F32) for _ in range(heads)]
    suffix_blk = {}
    for b in range(blocks):
        sums_t = jnp.concatenate([sums[:, b * rows_blk:(b + 1) * rows_blk]] * 16, axis=0).T
        denom = jnp.sqrt(sums_t[:, 0:1] / width + EPS)
        inv = 1.0 / denom
        factor = sums_t[:, 4:5] / (denom * denom * denom * width)
        inv = jnp.broadcast_to(inv, (rows_blk, D))
        factor = jnp.broadcast_to(factor, (rows_blk, D))
        for h in range(heads):
            c = h * blocks + b
            m = mixed[c]
            gain = gain_ref[:, pl.ds(h * D, D)]
            up = up_ref[tile(h, b)].astype(F32)
            normed = m * inv
            out_ref[tile(h, b)] = (normed * gain).astype(BF16)
            gain_rows[h] = gain_rows[h] + jnp.sum((up * normed).reshape(rows_blk // 8, 8, D), axis=0)
            grad = gain * up * inv - m * factor
            gmix[c] = grad
            suffix_blk[h, b] = dot3(split(grad.T), split(solved[c]))
    put(ss, [sum(suffix_blk[h, b] for b in range(blocks)) for h in range(heads)] + gain_rows)
    scan_s.start(0)

    for c, (h, b) in enumerate(chains):
        key = k_ref[tile(h, b)]
        pair = split(gmix[c])
        score = split(jnp.where(lower, dot(side(pair), vt2[c]), 0.0))
        rhs = dot3(pair, split(assoc_all[h, b].T)) + dot(score[0], key) + dot(score[1], key)
        start_cg(c, rhs)
    solve(scan_s)

    pair_blk = {}
    for c, (h, b) in enumerate(chains):
        adj = x_s[c]
        gq_ref[tile(h, b)] = adj.astype(BF16)
        one = dot3(split(adj.T), split(solved[c]))
        pair_blk[h, b] = one + one.T
    put(ps, pack_sym([sum(pair_blk[h, b] for b in range(blocks)) for h in range(heads)]))
    scan_p.start(0)

    gain_total = scan_s.total()
    for h in range(heads):
        rows = gain_total[heads * D + 8 * h:heads * D + 8 * h + 8, :]
        gg_ref[:, pl.ds(h * D, D)] = jnp.sum(rows, axis=0, keepdims=True)

    done = 0
    for h in range(heads):
        run = se[pl.ds(h * D, D), :]
        for b in reversed(range(blocks)):
            c = h * blocks + b
            key = k_ref[tile(h, b)]
            value = v_ref[tile(h, b)]
            sol, adj, grad = split(solved[c]), split(x_s[c]), split(gmix[c])
            key_sol = split(jnp.where(upper, dot_rows(k2[c], side(sol)), 0.0))
            cross = split(jnp.where(
                upper,
                dot_rows(side([value, value]), side(grad)) - dot_rows(k2[c], side(adj)),
                0.0,
            ))
            suf = split(run)
            suf_t = split(run.T)
            gv = dot(key, suf_t[0]) + dot(key, suf_t[1]) + dot3(key_sol, grad)
            gv_ref[tile(h, b)] = gv.astype(BF16)
            gk_loc[c] = (
                dot(value, suf[0]) + dot(value, suf[1]) + dot3(cross, sol) - dot3(key_sol, adj)
            )
            run = run + suffix_blk[h, b]
            if done < rounds:
                scan_p.finish(done)
                done += 1
    while done < rounds:
        scan_p.finish(done)
        done += 1
    pairs = unpack_sym(pe, heads)
    for h in range(heads):
        run = pairs[h]
        for b in reversed(range(blocks)):
            c = h * blocks + b
            key = k_ref[tile(h, b)]
            high, low = split(run)
            gk_ref[tile(h, b)] = (gk_loc[c] - dot(key, high) - dot(key, low)).astype(BF16)
            run = run + pair_blk[h, b]


def per_device(n_seq, n_head, queries, keys, values, ridge, gain, grad_out):
    tok = queries.shape[0]
    heads = ridge.shape[0]
    rounds = n_seq.bit_length() - 1
    chains = heads * (tok // BLOCK_ROWS)
    rows = BLOCK_ROWS
    sym = sym_rows(heads)
    suf = heads * (D + 8)
    vm = pltpu.VMEM

    def state(count):
        return [vm((rounds, count, D), F32), vm((rounds, count, D), F32), vm((count, D), F32)]

    big = [vm((chains, rows, D), F32)] * 9
    wide = jax.ShapeDtypeStruct((tok, heads * D), BF16)
    spec = pl.BlockSpec(memory_space=pltpu.VMEM)
    outs = pl.pallas_call(
        functools.partial(kernel, n_seq, n_head, heads, tok),
        out_shape=[wide, wide, wide, wide, jax.ShapeDtypeStruct((1, heads * D), F32)],
        in_specs=[spec, spec, spec, pl.BlockSpec(memory_space=pltpu.SMEM), spec, spec],
        out_specs=[spec] * 5,
        scratch_shapes=[
            vm((chains, 2 * D, rows), BF16),
            vm((chains, 2 * D, rows), BF16),
            vm((chains, rows, 2 * D), BF16),
            vm((chains, 2 * D, D), BF16),
            vm((chains, D, D), BF16),
        ]
        + big
        + state(sym) + state(heads * D) + state(suf) + state(sym)
        + [
            vm((8, tok), F32),
            vm((n_head - 1, 8, tok), F32),
            pltpu.SemaphoreType.DMA((4, rounds)),
            pltpu.SemaphoreType.DMA((4, rounds)),
            pltpu.SemaphoreType.DMA((n_head - 1,)),
            pltpu.SemaphoreType.DMA((n_head - 1,)),
        ],
        compiler_params=pltpu.CompilerParams(
            collective_id=0, has_side_effects=True, vmem_limit_bytes=40 * 2**20
        ),
    )(queries, keys, values, ridge, gain.reshape(1, -1), grad_out)
    return (*outs[:4], outs[4].reshape(-1))


def solution(mesh):
    n_seq, n_head = mesh.shape["seq"], mesh.shape["head"]
    wide = P("seq", "head")
    return jax.shard_map(
        functools.partial(per_device, n_seq, n_head),
        mesh=mesh,
        in_specs=(wide, wide, wide, P("head"), P("head"), wide),
        out_specs=(wide, wide, wide, wide, P("head")),
        check_vma=False,
    )
```

profile of v0, /device:TPU:0, one launch (start us, length us, event | category | flops | bytes accessed | tf_op | source)
XLA Modules:
  0.0 72.8 jit_solution(15436274016449047533)
XLA Ops:
  0.6 0.0 copy-start.4
  0.6 0.0 copy-start.5
  0.7 0.7 copy-done.4
  1.3 0.0 copy-done.5
  1.3 0.0 copy-start
  1.3 0.9 %copy-done = bf16[512,256]{1,0:T(8,128)(2,1)S(1)} copy-done((bf16[512,256]{1,0:T(8,128)(2,1)S(1)}, bf16[512,256]{1,0:T(8,128)(2,1)}, u32[]{:S(2)}) %copy-start) | copy-done | bytes 262168
  2.3 0.0 copy-start.1
  2.3 0.9 %copy-done.1 = bf16[512,256]{1,0:T(8,128)(2,1)S(1)} copy-done((bf16[512,256]{1,0:T(8,128)(2,1)S(1)}, bf16[512,256]{1,0:T(8,128)(2,1)}, u32[]{:S(2)}) %copy-start.1) | copy-done | bytes 262168
  3.2 0.0 copy-start.2
  3.2 0.9 %copy-done.2 = bf16[512,256]{1,0:T(8,128)(2,1)S(1)} copy-done((bf16[512,256]{1,0:T(8,128)(2,1)S(1)}, bf16[512,256]{1,0:T(8,128)(2,1)}, u32[]{:S(2)}) %copy-start.2) | copy-done | bytes 262168
  4.2 0.0 copy-start.3
  4.2 0.9 %copy-done.3 = bf16[512,256]{1,0:T(8,128)(2,1)S(1)} copy-done((bf16[512,256]{1,0:T(8,128)(2,1)S(1)}, bf16[512,256]{1,0:T(8,128)(2,1)}, u32[]{:S(2)}) %copy-start.3) | copy-done | bytes 262168
  5.1 64.3 %shard_map.101 = (bf16[512,256]{1,0:T(8,128)(2,1)S(1)}, bf16[512,256]{1,0:T(8,128)(2,1)S(1)}, bf16[512,256]{1,0:T(8,128)(2,1)S(1)}, bf16[512,256]{1,0:T(8,128)(2,1)S(1)}, f32[1,256]{1,0:T(1,128)S(1)}) custom-call(bf16[512,256]{1,0:T(8,128)(2,1)S(1)} %copy-done, bf16[512,256]{1,0:T(8,128)(2,1)S(1)} %copy-done.1, bf16[512,256]{1,0:T(8,128)(2,1)S(1)} %copy-done.2, ...), custom_call_target="tpu_custom_call" | custom-call | tf_op jit(solution)/shard_map/pallas_call | solution.py:385
  69.5 0.7 copy.16
  70.2 0.7 copy.17
  70.9 0.7 copy.18
  71.6 0.7 copy.19
  72.3 0.6 copy.20
Async XLA Ops:
  0.6 0.7 copy-start.4
  0.6 0.7 copy-start.5
  1.3 1.0 %copy-start = (bf16[512,256]{1,0:T(8,128)(2,1)S(1)}, bf16[512,256]{1,0:T(8,128)(2,1)}, u32[]{:S(2)}) copy-start(bf16[512,256]{1,0:T(8,128)(2,1)} %q_ref.1) | copy-start | bytes 786436
  2.3 0.9 %copy-start.1 = (bf16[512,256]{1,0:T(8,128)(2,1)S(1)}, bf16[512,256]{1,0:T(8,128)(2,1)}, u32[]{:S(2)}) copy-start(bf16[512,256]{1,0:T(8,128)(2,1)} %k_ref.1) | copy-start | bytes 786436
  3.2 0.9 %copy-start.2 = (bf16[512,256]{1,0:T(8,128)(2,1)S(1)}, bf16[512,256]{1,0:T(8,128)(2,1)}, u32[]{:S(2)}) copy-start(bf16[512,256]{1,0:T(8,128)(2,1)} %v_ref.1) | copy-start | bytes 786436
  4.2 0.9 %copy-start.3 = (bf16[512,256]{1,0:T(8,128)(2,1)S(1)}, bf16[512,256]{1,0:T(8,128)(2,1)}, u32[]{:S(2)}) copy-start(bf16[512,256]{1,0:T(8,128)(2,1)} %up_ref.1) | copy-start | bytes 786436
where the time goes:
time: 73.1 us; the launch traced here: 72.8 us
  Pallas kernels  64.3 us (88%)
  local copies, waits for them, and re-layouts  7.84 us (11%)
    pallas_call x1, Pallas kernels, per_device(): pl.pallas_call(functools.partial(kernel, n_seq, n_head, heads, tok), out_...  64.3 us
    unnamed x17, local copies, waits for them, and re-layouts  7.84 us

commit v1 on v0

--- a/solution.py
+++ b/solution.py
@@ -124,14 +124,23 @@
 
 def kernel(
     n_seq, n_head, heads, tok,
-    q_ref, k_ref, v_ref, ridge_ref, gain_ref, up_ref,
+    q_hbm, k_hbm, v_hbm, ridge_ref, gain_ref, up_hbm,
     out_ref, gq_ref, gk_ref, gv_ref, gg_ref,
+    q_ref, k_ref, v_ref, up_ref,
     kt2, vt2, k2, gram_h, gram_l,
     x_s, r_s, p_s, n_s, solved, mixed, gmix, gk_loc, gv_loc,
     gs, gr, ge, as_, ar, ae, ss, sr, se, ps, pr, pe,
     hs, hr,
-    sem_s, sem_r, hsem_s, hsem_r,
+    sem_s, sem_r, hsem_s, hsem_r, in_sem,
 ):
+    loads = [
+        pltpu.make_async_copy(src, dst, in_sem.at[i])
+        for i, (src, dst) in enumerate(
+            [(k_hbm, k_ref), (v_hbm, v_ref), (q_hbm, q_ref), (up_hbm, up_ref)]
+        )
+    ]
+    for load in loads:
+        load.start()
     rows_blk = BLOCK_ROWS
     blocks = tok // rows_blk
     chains = [(h, b) for h in range(heads) for b in range(blocks)]
@@ -153,6 +162,8 @@
     def tile(h, b):
         return (pl.ds(b * rows_blk, rows_blk), pl.ds(h * D, D))
 
+    loads[0].wait()
+    loads[1].wait()
     gram_blk, assoc_blk = {}, {}
     for c, (h, b) in enumerate(chains):
         key = k_ref[tile(h, b)]
@@ -175,6 +186,7 @@
         p_s[c] = rhs
         n_s[c] = jnp.broadcast_to(jnp.sum(rhs * rhs, axis=-1, keepdims=True), rhs.shape)
 
+    loads[2].wait()
     for c, (h, b) in enumerate(chains):
         start_cg(c, q_ref[tile(h, b)].astype(F32))
     for r in range(rounds):
@@ -234,6 +246,7 @@
                 scan.finish(r)
 
     solve(scan_a)
+    loads[3].wait()
 
     assoc_all = {}
     for h in range(heads):
@@ -366,6 +379,18 @@
             run = run + pair_blk[h, b]
 
 
+def hand_over(*refs):
+    sources, targets, sem = refs[:5], refs[5:10], refs[10]
+    copies = [
+        pltpu.make_async_copy(src, dst, sem.at[i])
+        for i, (src, dst) in enumerate(zip(sources, targets))
+    ]
+    for copy in copies:
+        copy.start()
+    for copy in copies:
+        copy.wait()
+
+
 def per_device(n_seq, n_head, queries, keys, values, ridge, gain, grad_out):
     tok = queries.shape[0]
     heads = ridge.shape[0]
@@ -382,12 +407,15 @@
     big = [vm((chains, rows, D), F32)] * 9
     wide = jax.ShapeDtypeStruct((tok, heads * D), BF16)
     spec = pl.BlockSpec(memory_space=pltpu.VMEM)
+    far = pl.BlockSpec(memory_space=pl.ANY)
+    near = vm((tok, heads * D), BF16)
     outs = pl.pallas_call(
         functools.partial(kernel, n_seq, n_head, heads, tok),
         out_shape=[wide, wide, wide, wide, jax.ShapeDtypeStruct((1, heads * D), F32)],
-        in_specs=[spec, spec, spec, pl.BlockSpec(memory_space=pltpu.SMEM), spec, spec],
+        in_specs=[far, far, far, pl.BlockSpec(memory_space=pltpu.SMEM), spec, far],
         out_specs=[spec] * 5,
         scratch_shapes=[
+            near, near, near, near,
             vm((chains, 2 * D, rows), BF16),
             vm((chains, 2 * D, rows), BF16),
             vm((chains, rows, 2 * D), BF16),
@@ -403,11 +431,20 @@
             pltpu.SemaphoreType.DMA((4, rounds)),
             pltpu.SemaphoreType.DMA((n_head - 1,)),
             pltpu.SemaphoreType.DMA((n_head - 1,)),
+            pltpu.SemaphoreType.DMA((4,)),
         ],
         compiler_params=pltpu.CompilerParams(
-            collective_id=0, has_side_effects=True, vmem_limit_bytes=40 * 2**20
+            collective_id=0, has_side_effects=True, vmem_limit_bytes=63 * 2**20
         ),
     )(queries, keys, values, ridge, gain.reshape(1, -1), grad_out)
+    outs = pl.pallas_call(
+        hand_over,
+        out_shape=[jax.ShapeDtypeStruct(x.shape, x.dtype) for x in outs],
+        in_specs=[far] * 5,
+        out_specs=[far] * 5,
+        scratch_shapes=[pltpu.SemaphoreType.DMA((5,))],
+        compiler_params=pltpu.CompilerParams(vmem_limit_bytes=63 * 2**20),
+    )(*outs)
     return (*outs[:4], outs[4].reshape(-1))
 
 

time: 73.1 us -> 98.6 us (1.35)
  Pallas kernels: 64.3 us -> 97.7 us
  local copies, waits for them, and re-layouts: 7.84 us -> 0 us
    pallas_call x0 -> x1, Pallas kernels: none -> 32.9 us  [per_device(): pl.pallas_call(hand_over, out_shape=[jax.ShapeDtypeStruct(x.shape, x.dtyp...]
    unnamed x17 -> x0, local copies, waits for them, and re-layouts: 7.84 us -> none
where the time goes in v1:
time: 98.6 us; the launch traced here: 98.4 us
  Pallas kernels  97.7 us (99%)
    pallas_call x1, Pallas kernels, per_device(): pl.pallas_call(functools.partial(kernel, n_seq, n_head, heads, tok), out_...  64.8 us
    pallas_call x1, Pallas kernels, per_device(): pl.pallas_call(hand_over, out_shape=[jax.ShapeDtypeStruct(x.shape, x.dtyp...  32.9 us

profile of v1, /device:TPU:0, one launch (start us, length us, event | category | flops | bytes accessed | tf_op | source)
XLA Modules:
  0.0 98.4 jit_solution(18218357742778963361)
XLA Ops:
  0.6 64.8 %shard_map.101 = (bf16[512,256]{1,0:T(8,128)(2,1)}, bf16[512,256]{1,0:T(8,128)(2,1)}, bf16[512,256]{1,0:T(8,128)(2,1)}, bf16[512,256]{1,0:T(8,128)(2,1)}, f32[1,256]{1,0:T(1,128)}) custom-call(bf16[512,256]{1,0:T(8,128)(2,1)} %q_hbm.1, bf16[512,256]{1,0:T(8,128)(2,1)} %k_hbm.1, bf16[512,256]{1,0:T(8,128)(2,1)} %v_hbm.1, f32[2]{0:T(128)} %ridge_ref.1, ...), custom_call_target="tpu_custom_call" | custom-call | tf_op jit(solution)/shard_map/pallas_call | solution.py:412
  65.4 32.9 %shard_map.102 = (bf16[512,256]{1,0:T(8,128)(2,1)}, bf16[512,256]{1,0:T(8,128)(2,1)}, bf16[512,256]{1,0:T(8,128)(2,1)}, bf16[512,256]{1,0:T(8,128)(2,1)}, f32[1,256]{1,0:T(1,128)}) custom-call(bf16[512,256]{1,0:T(8,128)(2,1)} %get-tuple-element.15.refs_0_, bf16[512,256]{1,0:T(8,128)(2,1)} %get-tuple-element.16.refs_1_, ...), custom_call_target="tpu_custom_call" | custom-call | tf_op jit(solution)/shard_map/pallas_call | solution.py:440

commit v2 on v0

--- a/solution.py
+++ b/solution.py
@@ -158,9 +158,7 @@
         key = k_ref[tile(h, b)]
         value = v_ref[tile(h, b)]
         key_t = key.astype(F32).T.astype(BF16)
-        value_t = value.astype(F32).T.astype(BF16)
         kt2[c] = jnp.concatenate([key_t, key_t], axis=0)
-        vt2[c] = jnp.concatenate([value_t, value_t], axis=0)
         k2[c] = side([key, key])
         both = dot(key_t, side([key, value]))
         gram_blk[h, b], assoc_blk[h, b] = both[:, :D], both[:, D:]
@@ -177,6 +175,8 @@
 
     for c, (h, b) in enumerate(chains):
         start_cg(c, q_ref[tile(h, b)].astype(F32))
+        value_t = v_ref[tile(h, b)].astype(F32).T.astype(BF16)
+        vt2[c] = jnp.concatenate([value_t, value_t], axis=0)
     for r in range(rounds):
         scan_g.finish(r)
     scan_a.start(0)
@@ -194,7 +194,7 @@
     lower = ri >= ci
     upper = ri <= ci
 
-    def cg_step(c, h, b):
+    def cg_step(c, h, b, last=False):
         p = p_s[c]
         pair = split(p)
         p2 = side(pair)
@@ -207,6 +207,8 @@
         now = n_s[c]
         alpha = now / (jnp.sum(p * image, axis=-1, keepdims=True) + EPS)
         x_s[c] = x_s[c] + alpha * p
+        if last:
+            return
         res = r_s[c] - alpha * image
         new = jnp.broadcast_to(jnp.sum(res * res, axis=-1, keepdims=True), p.shape)
         r_s[c] = res
@@ -220,7 +222,7 @@
             for c, (h, b) in enumerate(chains):
                 cg_step(c, h, b)
             for r in range(rounds):
-                if spacing * (r + 1) <= CG_STEPS:
+                if spacing * (r + 1) < CG_STEPS:
 
                     @pl.when(step == spacing * (r + 1) - 1)
                     def _():
@@ -228,9 +230,11 @@
 
             return carry
 
-        lax.fori_loop(0, CG_STEPS, step_fn, 0)
+        lax.fori_loop(0, CG_STEPS - 1, step_fn, 0)
+        for c, (h, b) in enumerate(chains):
+            cg_step(c, h, b, last=True)
         for r in range(rounds):
-            if spacing * (r + 1) > CG_STEPS:
+            if spacing * (r + 1) >= CG_STEPS:
                 scan.finish(r)
 
     solve(scan_a)

time: 73.1 us -> 72.9 us (level)
  no operation moved by 1% of the time
where the time goes in v2:
time: 72.9 us; the launch traced here: 72.7 us
  Pallas kernels  64.2 us (88%)
  local copies, waits for them, and re-layouts  7.84 us (11%)
    pallas_call x1, Pallas kernels, per_device(): pl.pallas_call(functools.partial(kernel, n_seq, n_head, heads, tok), out_...  64.2 us
    unnamed x17, local copies, waits for them, and re-layouts  7.84 us

profile of v2, /device:TPU:0, one launch (start us, length us, event | category | flops | bytes accessed | tf_op | source)
XLA Modules:
  0.0 72.7 jit_solution(4055562067974828644)
XLA Ops:
  0.6 0.0 copy-start.4
  0.6 0.0 copy-start.5
  0.7 0.7 copy-done.4
  1.3 0.0 copy-done.5
  1.3 0.0 copy-start
  1.3 0.9 %copy-done = bf16[512,256]{1,0:T(8,128)(2,1)S(1)} copy-done((bf16[512,256]{1,0:T(8,128)(2,1)S(1)}, bf16[512,256]{1,0:T(8,128)(2,1)}, u32[]{:S(2)}) %copy-start) | copy-done | bytes 262168
  2.3 0.0 copy-start.1
  2.3 0.9 %copy-done.1 = bf16[512,256]{1,0:T(8,128)(2,1)S(1)} copy-done((bf16[512,256]{1,0:T(8,128)(2,1)S(1)}, bf16[512,256]{1,0:T(8,128)(2,1)}, u32[]{:S(2)}) %copy-start.1) | copy-done | bytes 262168
  3.2 0.0 copy-start.2
  3.2 0.9 %copy-done.2 = bf16[512,256]{1,0:T(8,128)(2,1)S(1)} copy-done((bf16[512,256]{1,0:T(8,128)(2,1)S(1)}, bf16[512,256]{1,0:T(8,128)(2,1)}, u32[]{:S(2)}) %copy-start.2) | copy-done | bytes 262168
  4.2 0.0 copy-start.3
  4.2 0.9 %copy-done.3 = bf16[512,256]{1,0:T(8,128)(2,1)S(1)} copy-done((bf16[512,256]{1,0:T(8,128)(2,1)S(1)}, bf16[512,256]{1,0:T(8,128)(2,1)}, u32[]{:S(2)}) %copy-start.3) | copy-done | bytes 262168
  5.1 64.2 %shard_map.101 = (bf16[512,256]{1,0:T(8,128)(2,1)S(1)}, bf16[512,256]{1,0:T(8,128)(2,1)S(1)}, bf16[512,256]{1,0:T(8,128)(2,1)S(1)}, bf16[512,256]{1,0:T(8,128)(2,1)S(1)}, f32[1,256]{1,0:T(1,128)S(1)}) custom-call(bf16[512,256]{1,0:T(8,128)(2,1)S(1)} %copy-done, bf16[512,256]{1,0:T(8,128)(2,1)S(1)} %copy-done.1, bf16[512,256]{1,0:T(8,128)(2,1)S(1)} %copy-done.2, ...), custom_call_target="tpu_custom_call" | custom-call | tf_op jit(solution)/shard_map/pallas_call | solution.py:389
  69.3 0.7 copy.16
  70.0 0.7 copy.17
  70.7 0.7 copy.18
  71.4 0.7 copy.19
  72.1 0.6 copy.20
Async XLA Ops:
  0.6 0.7 copy-start.4
  0.6 0.7 copy-start.5
  1.3 1.0 %copy-start = (bf16[512,256]{1,0:T(8,128)(2,1)S(1)}, bf16[512,256]{1,0:T(8,128)(2,1)}, u32[]{:S(2)}) copy-start(bf16[512,256]{1,0:T(8,128)(2,1)} %q_ref.1) | copy-start | bytes 786436
  2.3 0.9 %copy-start.1 = (bf16[512,256]{1,0:T(8,128)(2,1)S(1)}, bf16[512,256]{1,0:T(8,128)(2,1)}, u32[]{:S(2)}) copy-start(bf16[512,256]{1,0:T(8,128)(2,1)} %k_ref.1) | copy-start | bytes 786436
  3.2 0.9 %copy-start.2 = (bf16[512,256]{1,0:T(8,128)(2,1)S(1)}, bf16[512,256]{1,0:T(8,128)(2,1)}, u32[]{:S(2)}) copy-start(bf16[512,256]{1,0:T(8,128)(2,1)} %v_ref.1) | copy-start | bytes 786436
  4.2 0.9 %copy-start.3 = (bf16[512,256]{1,0:T(8,128)(2,1)S(1)}, bf16[512,256]{1,0:T(8,128)(2,1)}, u32[]{:S(2)}) copy-start(bf16[512,256]{1,0:T(8,128)(2,1)} %up_ref.1) | copy-start | bytes 786436
